TPU v7x, 32 devices: a whole 2x2x4 slice. The times are simulated.
32 devices in a mesh: gx: 16 (over z, x, core), yz: 2 (over y).
Axes of the slice: x: 2, y: 2, z: 4, core: 2. Of those that a mesh axis runs over, the one named last changes fastest.
Arguments:
- conformation: float32 [3, 64, 384, 1024], P(None, 'gx', 'yz'), may hold values from -0.49 to 2.5, as said below
- velocity: float32 [3, 64, 384, 1024], P(None, 'gx', 'yz'), may hold values from -6 to 6
Outputs:
- updated: float32 [3, 64, 384, 1024], P(None, 'gx', 'yz')
Inputs may be any that keep to these rules, and one draw needn't show every extreme that they name: `conformation`: components 0 and 2 (c_xx, c_yy) lie in [0.5, 2.5] and component 1 (c_xy) in [-0.49, 0.49].
All inputs are finite; a program needn't handle non-finite values.
Results may differ from a plain program's by a relative error of at most 0.000076.
Values sent between devices are 32-bit elements; how exact they have to be, the bound alone decides.
No kernel may reach another device: no remote copies, remote signals or barrier semaphores. Data moves between devices by JAX's collectives and lax.ppermute only.
A program may use at most 256 MiB of HBM per device.

v0:
```python
import math
import jax
import jax.numpy as jnp
from jax import lax
from jax.sharding import PartitionSpec as P

stencil_coeffs = (0.8, -0.2, 4.0 / 105.0, -1.0 / 280.0)
extensibility = 10.0
relax_rate = 1.0 / 0.04
courant = 0.5


def padded_2(x, sides, width):
    for axis, dim in sides:
        count, length = (lax.axis_size(axis), x.shape[dim])
        up = [(i, (i + 1) % count) for i in range(count)]
        down = [(j, i) for i, j in up]
        last = lax.slice_in_dim(x, length - width, length, axis=dim)
        initial = lax.slice_in_dim(x, 0, width, axis=dim)
        before = lax.ppermute(last, axis, up)
        after = lax.ppermute(initial, axis, down)
        x = jnp.concatenate([before, x, after], axis=dim)
    return x


def storage_points(count, groups):
    index = jnp.arange(count, dtype=jnp.int32)
    per_group = count // groups
    return index % per_group * groups + index // per_group


def cheb_matrix(count, points):
    last = count - 1
    half_step = math.pi / (2.0 * last)
    weights = jnp.where((points == 0) | (points == last), 2.0, 1.0).astype(jnp.float32)
    same = points[:, None] == points[None, :]
    sums = (points[:, None] + points[None, :]).astype(jnp.float32) * half_step
    diffs = (points[:, None] - points[None, :]).astype(jnp.float32) * half_step
    signs = (1 - 2 * ((points[:, None] + points[None, :]) % 2)).astype(jnp.float32)
    apart = -2.0 * jnp.sin(sums) * jnp.sin(diffs)
    safe = jnp.where(same, 1.0, apart)
    offdiag = jnp.where(same, 0.0, weights[:, None] / weights[None, :] * signs / safe)
    return offdiag - jnp.diag(jnp.sum(offdiag, axis=1))


def centered(padded, width, count, axis, spacing):
    total = jnp.zeros_like(lax.slice_in_dim(padded, width, width + count, axis=axis))
    for offset, coeff in enumerate(stencil_coeffs, start=1):
        ahead = lax.slice_in_dim(padded, width + offset, width + offset + count, axis=axis)
        behind = lax.slice_in_dim(padded, width - offset, width - offset + count, axis=axis)
        total = total + coeff * (ahead - behind)
    return total / spacing


def wall_terms(comp, vel_v, dy_comp, dy_u, dy_v):
    term_xx = -vel_v * dy_comp[0] + 2.0 * dy_u * comp[1]
    term_xy = -vel_v * dy_comp[1] + dy_u * comp[2] + dy_v * comp[1]
    term_yy = -vel_v * dy_comp[2] + 2.0 * dy_v * comp[2]
    return jnp.stack([term_xx, term_xy, term_yy])


def local_terms(comp, vel, along_x, along_z):
    peterlin = (extensibility - 2.0) / (extensibility - comp[0] - comp[2])
    grad_ux = along_x[3]
    grad_vx = along_x[4]
    term_xx = (
        -vel[0] * along_x[0]
        - vel[2] * along_z[0]
        + 2.0 * grad_ux * comp[0]
        - relax_rate * (peterlin * comp[0] - 1.0)
    )
    term_xy = (
        -vel[0] * along_x[1]
        - vel[2] * along_z[1]
        + grad_ux * comp[1]
        + grad_vx * comp[0]
        - relax_rate * peterlin * comp[1]
    )
    term_yy = (
        -vel[0] * along_x[2]
        - vel[2] * along_z[2]
        + 2.0 * grad_vx * comp[1]
        - relax_rate * (peterlin * comp[2] - 1.0)
    )
    return jnp.stack([term_xx, term_xy, term_yy])


def shards(conformation, velocity):
    planes = conformation.shape[1]
    local_rows = conformation.shape[2]
    groups = lax.axis_size("yz")
    count = local_rows * groups
    spacing = math.pi / (count - 1)
    points = storage_points(count, groups)
    cheb = cheb_matrix(count, points)
    points_here = jnp.arange(local_rows, dtype=jnp.int32) * groups + lax.axis_index("yz")
    theta = math.pi * points_here.astype(jnp.float32) / (count - 1)
    step_size = courant * spacing * (jnp.sin(theta) + spacing)
    block = jnp.concatenate([conformation, velocity[0:2]], axis=0)
    derived = jnp.einsum(
        "ij,fkjz->fkiz",
        cheb,
        lax.all_to_all(block, "yz", split_axis=3, concat_axis=2, tiled=True),
        precision=lax.Precision.HIGHEST,
    )
    returned_back = lax.all_to_all(derived, "yz", split_axis=2, concat_axis=3, tiled=True)
    yterms = wall_terms(
        conformation, velocity[1], returned_back[0:3], returned_back[3], returned_back[4]
    )
    padded = padded_2(block, (("gx", 1),), 4)
    along_x = centered(padded, 4, planes, 1, spacing)
    padded_z = jnp.pad(conformation, ((0, 0), (0, 0), (0, 0), (4, 4)), mode="wrap")
    along_z = centered(padded_z, 4, conformation.shape[3], 3, spacing)
    other = local_terms(conformation, velocity, along_x, along_z)
    return conformation + step_size[None, None, :, None] * (other + yterms)


def solution(mesh):
    in_specs = (P(None, "gx", "yz", None), P(None, "gx", "yz", None))
    out_specs = P(None, "gx", "yz", None)
    return jax.shard_map(shards, mesh=mesh, in_specs=in_specs, out_specs=out_specs, check_vma=False)
```

profile of v0, /device:TPU:16, one launch (start us, length us, event | category | flops | bytes accessed | tf_op | source)
XLA Modules:
  0.0 632.3 jit_solution(1645302906625651038)
XLA Ops:
  0.0 3.5 slice.149
  3.5 2.0 copy-done
  5.5 6.6 %pad_maximum_fusion.1 = f32[5,4,192,1024]{3,2,1,0:T(8,128)} fusion(f32[2,4,192,1024]{3,2,1,0:T(8,128)S(1)} %slice.149, f32[3,4,192,1024]{3,2,1,0:T(8,128)S(1)} %copy-done), kind=kLoop, calls=%fused_computation.18 | loop fusion | flops 3932160 | bytes 31457280 | tf_op jit(solution)/shard_map/concatenate | solution.py:99
  12.1 0.8 copy-done.2
  12.9 0.8 collective-permute-start
  13.7 21.9 %copy.19 = f32[5,4,192,1024]{2,1,0,3:T(4,128)} copy(f32[5,4,192,1024]{3,2,1,0:T(8,128)} %pad_maximum_fusion.1) | data formatting | bytes 31457280 | tf_op jit(solution)/shard_map/concatenate | solution.py:99
  35.6 11.2 %all-to-all-start = ((f32[5,4,192,1024]{2,1,0,3:T(4,128)}), f32[5,4,192,1024]{2,1,0,3:T(4,128)}, u32[]{:S(2)}, u32[]{:S(2)}) async-start(f32[5,4,192,1024]{2,1,0,3:T(4,128)} %copy.19), calls=%async_computation | async-start | bytes 41943040 | tf_op jit(solution)/shard_map/all_to_all | solution.py:103
  46.8 0.6 add_multiply_fusion
  47.5 2.0 fusion.68
  49.5 4.8 fusion.51
  54.3 4.4 fusion.73
  58.8 36.0 %fusion.12 = f32[3,4,192,1024]{3,2,1,0:T(8,128)} fusion(f32[3,4,192,1024]{3,2,1,0:T(8,128)} %param.2, f32[3,4,192,4]{3,2,1,0:T(8,128)S(1)} %get-tuple-element.18, f32[3,4,192,4]{3,2,1,0:T(8,128)S(1)} %get-tuple-element.17), kind=kLoop, calls=%fused_computation.30 | loop fusion | flops 47185920 | bytes 18948096 | tf_op jit(solution)/shard_map/div | solution.py:52
  94.8 180.4 %all-to-all-done = f32[5,4,192,1024]{2,1,0,3:T(4,128)} async-done(((f32[5,4,192,1024]{2,1,0,3:T(4,128)}), f32[5,4,192,1024]{2,1,0,3:T(4,128)}, u32[]{:S(2)}, u32[]{:S(2)}) %all-to-all-start) | async-done | bytes 15728672 | tf_op jit(solution)/shard_map/all_to_all | solution.py:103
  275.2 30.9 %copy.32 = f32[5,4,192,2,512]{4,3,2,1,0:T(2,128)} copy(f32[5,4,192,2,512]{2,1,0,4,3:T(4,128)} %bitcast) | data formatting | bytes 31457280 | tf_op jit(solution)/shard_map/all_to_all | solution.py:103
  306.2 14.0 %copy.21 = f32[5,4,2,192,512]{4,3,2,1,0:T(8,128)} copy(f32[5,4,2,192,512]{4,2,3,1,0:T(2,128)} %bitcast.39) | data formatting | bytes 31457280 | tf_op jit(solution)/shard_map/all_to_all | solution.py:103
  320.1 54.5 %convolution_bitcast_fusion = f32[5,4,384,512]{2,3,1,0:T(8,128)} fusion(f32[5,4,384,512]{3,2,1,0:T(8,128)} %bitcast.38, f32[384,384,1,1]{1,0,3,2:T(8,128)S(1)} %fusion.73), kind=kOutput, calls=%fused_computation.48 | convolution fusion | flops 18119393280 | bytes 32047104 | tf_op jit(solution)/shard_map/ij,fkjz->fkiz/dot_general | solution.py:100
  374.6 19.4 %copy.23 = f32[5,4,384,512]{3,1,0,2:T(4,128)} copy(f32[5,4,384,512]{2,3,1,0:T(8,128)} %convolution_bitcast_fusion) | data formatting | bytes 31457280 | tf_op jit(solution)/shard_map/ij,fkjz->fkiz/transpose | solution.py:100
  394.1 9.4 %all-to-all-start.1 = ((f32[5,4,384,512]{3,1,0,2:T(4,128)}), f32[5,4,384,512]{3,1,0,2:T(4,128)}, u32[]{:S(2)}, u32[]{:S(2)}) async-start(f32[5,4,384,512]{3,1,0,2:T(4,128)} %copy.23), calls=%async_computation.1 | async-start | bytes 31457280 | tf_op jit(solution)/shard_map/all_to_all | solution.py:106
  403.5 41.9 %pad_maximum_fusion = (f32[5,8,192,1024]{3,2,1,0:T(8,128)}, f32[5,8,192,1024]{3,2,1,0:T(8,128)}) fusion(f32[5,4,192,1024]{3,2,1,0:T(8,128)} %collective-permute-done, f32[2,4,192,1024]{3,2,1,0:T(8,128)} %copy-done.2, f32[3,4,192,1024]{3,2,1,0:T(8,128)} %param.2, f32[5,4,192,1024]{3,2,1,0:T(8,128)} %collective-permute-done.1), kind=kLoop, calls=%fused_computation | loop fusion | flops 31457280 | bytes 110100480 | tf_op jit(solution)/shard_map/concatenate | solution.py:22
  445.4 46.8 %fusion.3 = f32[5,4,192,1024]{3,2,1,0:T(8,128)} fusion(f32[5,8,192,1024]{3,2,1,0:T(8,128)} %get-tuple-element.16, f32[5,8,192,1024]{3,2,1,0:T(8,128)} %get-tuple-element.15, f32[5,4,192,1024]{3,2,1,0:T(8,128)} %collective-permute-done, f32[5,4,192,1024]{3,2,1,0:T(8,128)} %collective-permute-done.1), kind=kLoop, calls=%fused_computation.12 | loop fusion | flops 47185920 | bytes 141557760 | tf_op jit(solution)/shard_map/div | solution.py:52
  492.3 13.0 %fusion.33 = f32[1,4,192,1024]{3,2,1,0:T(8,128)} fusion(f32[3,4,192,1024]{3,2,1,0:T(8,128)} %fusion.12, f32[5,4,192,1024]{3,2,1,0:T(8,128)} %fusion.3, f32[3,4,192,1024]{3,2,1,0:T(8,128)} %param.2, f32[3,4,192,1024]{3,2,1,0:T(8,128)} %param.3), kind=kLoop, calls=%fused_computation.63 | loop fusion | flops 11010048 | bytes 31457280 | tf_op jit(solution)/shard_map/sub | solution.py:73
  505.2 1.8 copy-done.1
  507.0 11.3 %fusion.36 = (f32[1,4,192,1024]{3,2,1,0:T(8,128)}, f32[1,4,192,1024]{3,2,1,0:T(8,128)}) fusion(f32[3,4,192,1024]{3,2,1,0:T(8,128)} %fusion.12, f32[5,4,192,1024]{3,2,1,0:T(8,128)S(1)} %copy-done.1, f32[3,4,192,1024]{3,2,1,0:T(8,128)} %param.2, f32[3,4,192,1024]{3,2,1,0:T(8,128)} %param.3), kind=kLoop, calls=%fused_computation.68 | loop fusion | flops 18874368 | bytes 40894464 | tf_op jit(solution)/shard_map/sub | solution.py:67
  518.3 56.5 %all-to-all-done.1 = f32[5,4,384,512]{3,1,0,2:T(4,128)} async-done(((f32[5,4,384,512]{3,1,0,2:T(4,128)}), f32[5,4,384,512]{3,1,0,2:T(4,128)}, u32[]{:S(2)}, u32[]{:S(2)}) %all-to-all-start.1) | async-done | bytes 15728672 | tf_op jit(solution)/shard_map/all_to_all | solution.py:106
  574.9 15.8 %copy.24 = f32[5,4,384,512]{3,2,1,0:T(8,128)} copy(f32[5,4,384,512]{3,1,0,2:T(4,128)} %all-to-all-done.1) | data formatting | bytes 31457280 | tf_op jit(solution)/shard_map/all_to_all | solution.py:106
  590.7 11.9 %slice_bitcast_fusion.4 = (f32[1,4,2,24,8,512]{5,4,3,2,1,0:T(8,128)}, f32[1,4,2,24,8,512]{5,4,3,2,1,0:T(8,128)}, f32[1,4,2,24,8,512]{5,4,3,2,1,0:T(8,128)}, f32[...) fusion(f32[5,4,192,2,512]{4,2,3,1,0:T(8,128)} %bitcast.37), kind=kLoop, calls=%fused_computation.53 | loop fusion | bytes 31457280
  602.6 2.4 copy.33
  605.0 2.4 copy.34
  608.2 2.0 copy.37
  610.1 1.4 slice-done.1
  611.8 8.3 %multiply_add_fusion.2 = (f32[1,4,192,1024]{3,2,1,0:T(8,128)}, f32[1,4,192,1024]{3,2,1,0:T(8,128)}, f32[1,4,192,1024]{3,2,1,0:T(8,128)}) fusion(f32[1,4,192,1024]{3,2,1,0:T(8,128)S(1)} %bitcast.41, f32[1,4,192,1024]{3,2,1,0:T(8,128)S(1)} %bitcast.40, f32[3,4,192,1024]{3,2,1,0:T(8,128)S(1)} %bitcast.36, f32[3,4,192,1024]{3,2,1,0:T(8,128)} %param.3, ...), kind=kLoop, calls=%fused_computation.72 | loop fusion | flops 11010048 | bytes 34603008 | tf_op jit(solution)/shard_map/add | solution.py:56
  620.1 11.9 %fusion.26 = f32[3,4,192,1024]{3,2,1,0:T(8,128)} fusion(f32[3,4,192,1024]{3,2,1,0:T(8,128)S(1)} %bitcast.36, f32[1,4,192,1024]{3,2,1,0:T(8,128)} %get-tuple-element.6, f32[1,4,192,1024]{3,2,1,0:T(8,128)} %fusion.33, f32[1,4,192,1024]{3,2,1,0:T(8,128)} %get-tuple-element.5, f32[1,4,192,1024]{3,2,1,0:T(8,128)} %get-tuple-element.9, ...), kind=kLoop, calls=%fused_computation.47 | loop fusion | flops 16515072 | bytes 37749504 | tf_op jit(solution)/shard_map/add | solution.py:115
  (22 shorter events, 1.0 us)
Async XLA Ops:
  0.0 5.5 copy-start
  5.5 7.4 %copy-start.2 = (f32[2,4,192,1024]{3,2,1,0:T(8,128)}, f32[2,4,192,1024]{3,2,1,0:T(8,128)S(1)}, u32[]{:S(2)}) copy-start(f32[2,4,192,1024]{3,2,1,0:T(8,128)S(1)} %slice.149) | copy-start | bytes 18874372
  12.9 390.6 %collective-permute-start = (f32[5,4,192,1024]{3,2,1,0:T(8,128)}, f32[5,4,192,1024]{3,2,1,0:T(8,128)}, u32[]{:S(2)}, u32[]{:S(2)}) collective-permute-start(f32[5,4,192,1024]{3,2,1,0:T(8,128)} %pad_maximum_fusion.1), channel_id=1, source_target_pairs={{2,0},{4,2},{6,4},{8,6},{10,8},{12,10},{14,12},{16,14},{18,16},{20... | collective-permute-start | bytes 47185928 | tf_op jit(solution)/shard_map/ppermute | solution.py:21
  13.7 389.8 %collective-permute-start.1 = (f32[5,4,192,1024]{3,2,1,0:T(8,128)}, f32[5,4,192,1024]{3,2,1,0:T(8,128)}, u32[]{:S(2)}, u32[]{:S(2)}) collective-permute-start(f32[5,4,192,1024]{3,2,1,0:T(8,128)} %pad_maximum_fusion.1), channel_id=1, source_target_pairs={{0,2},{2,4},{4,6},{6,8},{8,10},{10,12},{12,14},{14,16},{16,18},{18... | collective-permute-start | bytes 47185928 | tf_op jit(solution)/shard_map/ppermute | solution.py:20
  35.6 239.6 %all-to-all-start = ((f32[5,4,192,1024]{2,1,0,3:T(4,128)}), f32[5,4,192,1024]{2,1,0,3:T(4,128)}, u32[]{:S(2)}, u32[]{:S(2)}) async-start(f32[5,4,192,1024]{2,1,0,3:T(4,128)} %copy.19), calls=%async_computation | async-start | bytes 41943040 | tf_op jit(solution)/shard_map/all_to_all | solution.py:103
  394.1 180.8 %all-to-all-start.1 = ((f32[5,4,384,512]{3,1,0,2:T(4,128)}), f32[5,4,384,512]{3,1,0,2:T(4,128)}, u32[]{:S(2)}, u32[]{:S(2)}) async-start(f32[5,4,384,512]{3,1,0,2:T(4,128)} %copy.23), calls=%async_computation.1 | async-start | bytes 31457280 | tf_op jit(solution)/shard_map/all_to_all | solution.py:106
  492.3 14.7 %copy-start.1 = (f32[5,4,192,1024]{3,2,1,0:T(8,128)S(1)}, f32[5,4,192,1024]{3,2,1,0:T(8,128)}, u32[]{:S(2)}) copy-start(f32[5,4,192,1024]{3,2,1,0:T(8,128)} %fusion.3) | copy-start | bytes 47185924
  602.6 5.2 copy-start.4
  605.0 3.2 copy-start.3
  605.0 5.2 slice-start
  607.4 4.2 slice-start.1
  607.8 4.0 slice-start.2
  611.8 8.4 %copy-start.5 = (f32[192]{0:T(256)S(1)}, f32[192]{0:T(256)}, u32[]{:S(2)}) copy-start(f32[192]{0:T(256)} %add_multiply_fusion) | copy-start | bytes 2308
where the time goes:
time: 641 us; the launch traced here: 632 us
  waiting for transfers between devices  237 us (37%)
  other arithmetic  186 us (29%)
  local copies, waits for them, and re-layouts  133 us (21%)
  matrix products  54.5 us (9%)
  starting transfers between devices  21.4 us (3%)
    all_to_all x1, waiting for transfers between devices, shards(): lax.all_to_all(block, 'yz', split_axis=3, concat_axis=2, tiled=True)  180 us
    div x2, other arithmetic, centered(): return total / spacing  82.8 us
    all_to_all x1, waiting for transfers between devices, shards(): lax.all_to_all(derived, 'yz', split_axis=2, concat_axis=3, tiled=True)  56.5 us
    dot_general x1, matrix products, shards(): jnp.einsum('ij,fkjz->fkiz', cheb, lax.all_to_all(block, 'yz', split_axis=...  54.5 us
    all_to_all x2, local copies, waits for them, and re-layouts, shards(): lax.all_to_all(block, 'yz', split_axis=3, concat_axis=2, tiled=True)  44.9 us
    concatenate x1, other arithmetic, padded_2(): x = jnp.concatenate([before, x, after], axis=dim)  41.9 us
    concatenate x1, local copies, waits for them, and re-layouts, shards(): block = jnp.concatenate([conformation, velocity[0:2]], axis=0)  21.9 us
    transpose x1, local copies, waits for them, and re-layouts, shards(): jnp.einsum('ij,fkjz->fkiz', cheb, lax.all_to_all(block, 'yz', split_axis=...  19.4 us
  transfers between devices with their start and end apart: 4, of which 2 were waited for; matrix products, arithmetic and copies ran while one was open for 48% of the time, Pallas kernels for 0%

commit v1 on v0

--- a/solution.py
+++ b/solution.py
@@ -103,7 +103,10 @@
         lax.all_to_all(block, "yz", split_axis=3, concat_axis=2, tiled=True),
         precision=lax.Precision.HIGHEST,
     )
-    returned_back = lax.all_to_all(derived, "yz", split_axis=2, concat_axis=3, tiled=True)
+    returned_back = jnp.concatenate(
+        lax.all_to_all(jnp.stack(jnp.split(derived, lax.axis_size("yz"), axis=2)), "yz", 0, 0),
+        axis=3,
+    )
     yterms = wall_terms(
         conformation, velocity[1], returned_back[0:3], returned_back[3], returned_back[4]
     )

time: 641 us -> 599 us (0.934)
  local copies, waits for them, and re-layouts: 133 us -> 89.5 us
  matrix products: 54.5 us -> 41.9 us
  other arithmetic: 186 us -> 195 us
    all_to_all x2 -> x1, local copies, waits for them, and re-layouts: 44.9 us -> 22.2 us  [shards(): lax.all_to_all(block, 'yz', split_axis=3, concat_axis=2, tiled=True)]
    transpose x1 -> x0, local copies, waits for them, and re-layouts: 19.4 us -> none  [shards(): jnp.einsum('ij,fkjz->fkiz', cheb, lax.all_to_all(block, 'yz', split_axis=...]
    all_to_all x1 -> x0, local copies, waits for them, and re-layouts: 15.8 us -> none  [shards(): lax.all_to_all(derived, 'yz', split_axis=2, concat_axis=3, tiled=True)]
    another operation x0 -> x1, local copies, waits for them, and re-layouts: none -> 14.3 us  [shards(): jnp.stack(jnp.split(derived, lax.axis_size('yz'), axis=2))]
    another operation x0 -> x1, other arithmetic: none -> 14.3 us  [shards(): jnp.stack(jnp.split(derived, lax.axis_size('yz'), axis=2))]
    dot_general x1, matrix products: 54.5 us -> 41.9 us  [shards(): jnp.einsum('ij,fkjz->fkiz', cheb, lax.all_to_all(block, 'yz', split_axis=...]
  transfers between devices with their start and end apart: 4 -> 4, of which waited for: 2 -> 2; matrix products, arithmetic and copies ran while one was open for 48% -> 46% of each run, Pallas kernels for 0% -> 0%
where the time goes in v1:
time: 599 us; the launch traced here: 590 us
  waiting for transfers between devices  242 us (40%)
  other arithmetic  195 us (33%)
  local copies, waits for them, and re-layouts  89.5 us (15%)
  matrix products  41.9 us (7%)
  starting transfers between devices  21.5 us (4%)
    all_to_all x1, waiting for transfers between devices, shards(): lax.all_to_all(block, 'yz', split_axis=3, concat_axis=2, tiled=True)  185 us
    div x2, other arithmetic, centered(): return total / spacing  82.7 us
    all_to_all x1, waiting for transfers between devices, shards(): lax.all_to_all(jnp.stack(jnp.split(derived, lax.axis_size('yz'), axis=2))...  56.7 us
    dot_general x1, matrix products, shards(): jnp.einsum('ij,fkjz->fkiz', cheb, lax.all_to_all(block, 'yz', split_axis=...  41.9 us
    concatenate x1, other arithmetic, padded_2(): x = jnp.concatenate([before, x, after], axis=dim)  41.7 us
    all_to_all x1, local copies, waits for them, and re-layouts, shards(): lax.all_to_all(block, 'yz', split_axis=3, concat_axis=2, tiled=True)  22.2 us
    concatenate x1, local copies, waits for them, and re-layouts, shards(): block = jnp.concatenate([conformation, velocity[0:2]], axis=0)  21.8 us
    unnamed x19, local copies, waits for them, and re-layouts  18.2 us
  transfers between devices with their start and end apart: 4, of which 2 were waited for; matrix products, arithmetic and copies ran while one was open for 46% of the time, Pallas kernels for 0%

profile of v1, /device:TPU:16, one launch (start us, length us, event | category | flops | bytes accessed | tf_op | source)
XLA Modules:
  0.0 590.2 jit_solution(8818032292267541309)
XLA Ops:
  0.0 3.5 slice.149
  3.5 2.0 copy-done
  5.5 6.6 %pad_maximum_fusion.1 = f32[5,4,192,1024]{3,2,1,0:T(8,128)} fusion(f32[2,4,192,1024]{3,2,1,0:T(8,128)S(1)} %slice.149, f32[3,4,192,1024]{3,2,1,0:T(8,128)S(1)} %copy-done), kind=kLoop, calls=%fused_computation.18 | loop fusion | flops 3932160 | bytes 31457280 | tf_op jit(solution)/shard_map/concatenate | solution.py:99
  12.1 0.8 copy-done.2
  12.9 0.8 collective-permute-start
  13.7 21.8 %copy.10 = f32[5,4,192,1024]{2,1,0,3:T(4,128)} copy(f32[5,4,192,1024]{3,2,1,0:T(8,128)} %pad_maximum_fusion.1) | data formatting | bytes 31457280 | tf_op jit(solution)/shard_map/concatenate | solution.py:99
  35.5 11.2 %all-to-all-start = ((f32[5,4,192,1024]{2,1,0,3:T(4,128)}), f32[5,4,192,1024]{2,1,0,3:T(4,128)}, u32[]{:S(2)}, u32[]{:S(2)}) async-start(f32[5,4,192,1024]{2,1,0,3:T(4,128)} %copy.10), calls=%async_computation | async-start | bytes 41943040 | tf_op jit(solution)/shard_map/all_to_all | solution.py:103
  46.7 0.6 add_multiply_fusion
  47.3 2.0 fusion.68
  49.3 4.8 fusion.51
  54.2 35.8 %fusion.12 = f32[3,4,192,1024]{3,2,1,0:T(8,128)} fusion(f32[3,4,192,1024]{3,2,1,0:T(8,128)} %param.2, f32[3,4,192,4]{3,2,1,0:T(8,128)S(1)} %get-tuple-element.20, f32[3,4,192,4]{3,2,1,0:T(8,128)S(1)} %get-tuple-element.19), kind=kLoop, calls=%fused_computation.31 | loop fusion | flops 47185920 | bytes 18948096 | tf_op jit(solution)/shard_map/div | solution.py:52
  90.0 185.1 %all-to-all-done = f32[5,4,192,1024]{2,1,0,3:T(4,128)} async-done(((f32[5,4,192,1024]{2,1,0,3:T(4,128)}), f32[5,4,192,1024]{2,1,0,3:T(4,128)}, u32[]{:S(2)}, u32[]{:S(2)}) %all-to-all-start) | async-done | bytes 15728672 | tf_op jit(solution)/shard_map/all_to_all | solution.py:103
  275.1 22.2 %copy.11 = f32[5,4,192,2,512]{4,2,3,1,0:T(8,128)} copy(f32[5,4,192,2,512]{2,1,0,4,3:T(4,128)} %bitcast) | data formatting | bytes 31457280 | tf_op jit(solution)/shard_map/all_to_all | solution.py:103
  297.2 41.9 %convolution_bitcast_fusion = f32[5,4,384,512]{3,2,1,0:T(8,128)} fusion(f32[5,4,384,512]{3,2,1,0:T(8,128)} %bitcast.34, f32[384]{0:T(512)S(1)} %fusion.51, f32[384]{0:T(512)S(1)} %or_select_fusion, s32[384]{0:T(512)S(1)} %fusion.56), kind=kOutput, calls=%fused_computation.49 | convolution fusion | flops 18123964416 | bytes 31461888 | tf_op jit(solution)/shard_map/ij,fkjz->fkiz/dot_general | solution.py:100
  339.1 14.3 %slice_bitcast_fusion.1 = (f32[1,5,4,192,512]{4,3,2,1,0:T(8,128)}, f32[1,5,4,192,512]{4,3,2,1,0:T(8,128)}) fusion(f32[5,4,384,512]{3,2,1,0:T(8,128)} %convolution_bitcast_fusion), kind=kLoop, calls=%fused_computation.51 | loop fusion | bytes 31457280 | tf_op jit(solution)/shard_map/stack | solution.py:107
  353.5 14.3 %pad_maximum_fusion.2 = f32[2,5,4,192,512]{4,3,2,1,0:T(8,128)} fusion(f32[1,5,4,192,512]{4,3,2,1,0:T(8,128)} %get-tuple-element.16, f32[1,5,4,192,512]{4,3,2,1,0:T(8,128)} %get-tuple-element.15), kind=kLoop, calls=%fused_computation.19 | loop fusion | flops 3932160 | bytes 31457280 | tf_op jit(solution)/shard_map/stack | solution.py:107
  367.8 9.5 %all-to-all-start.1 = ((f32[2,5,4,192,512]{4,3,2,1,0:T(8,128)}), f32[2,5,4,192,512]{4,3,2,1,0:T(8,128)}, u32[]{:S(2)}, u32[]{:S(2)}) async-start(f32[2,5,4,192,512]{4,3,2,1,0:T(8,128)} %pad_maximum_fusion.2), calls=%async_computation.1 | async-start | bytes 31457280 | tf_op jit(solution)/shard_map/all_to_all | solution.py:107
  377.3 41.7 %pad_maximum_fusion = (f32[5,8,192,1024]{3,2,1,0:T(8,128)}, f32[5,8,192,1024]{3,2,1,0:T(8,128)}) fusion(f32[5,4,192,1024]{3,2,1,0:T(8,128)} %collective-permute-done, f32[2,4,192,1024]{3,2,1,0:T(8,128)} %copy-done.2, f32[3,4,192,1024]{3,2,1,0:T(8,128)} %param.2, f32[5,4,192,1024]{3,2,1,0:T(8,128)} %collective-permute-done.1), kind=kLoop, calls=%fused_computation | loop fusion | flops 31457280 | bytes 110100480 | tf_op jit(solution)/shard_map/concatenate | solution.py:22
  419.0 46.8 %fusion.3 = f32[5,4,192,1024]{3,2,1,0:T(8,128)} fusion(f32[5,8,192,1024]{3,2,1,0:T(8,128)} %get-tuple-element.18, f32[5,8,192,1024]{3,2,1,0:T(8,128)} %get-tuple-element.17, f32[5,4,192,1024]{3,2,1,0:T(8,128)} %collective-permute-done, f32[5,4,192,1024]{3,2,1,0:T(8,128)} %collective-permute-done.1), kind=kLoop, calls=%fused_computation.12 | loop fusion | flops 47185920 | bytes 141557760 | tf_op jit(solution)/shard_map/div | solution.py:52
  465.8 12.9 %fusion.33 = f32[1,4,192,1024]{3,2,1,0:T(8,128)} fusion(f32[3,4,192,1024]{3,2,1,0:T(8,128)} %fusion.12, f32[5,4,192,1024]{3,2,1,0:T(8,128)} %fusion.3, f32[3,4,192,1024]{3,2,1,0:T(8,128)} %param.2, f32[3,4,192,1024]{3,2,1,0:T(8,128)} %param.3), kind=kLoop, calls=%fused_computation.66 | loop fusion | flops 11010048 | bytes 31457280 | tf_op jit(solution)/shard_map/sub | solution.py:73
  478.7 1.8 copy-done.1
  480.5 11.4 %fusion.36 = (f32[1,4,192,1024]{3,2,1,0:T(8,128)}, f32[1,4,192,1024]{3,2,1,0:T(8,128)}) fusion(f32[3,4,192,1024]{3,2,1,0:T(8,128)} %fusion.12, f32[5,4,192,1024]{3,2,1,0:T(8,128)S(1)} %copy-done.1, f32[3,4,192,1024]{3,2,1,0:T(8,128)} %param.2, f32[3,4,192,1024]{3,2,1,0:T(8,128)} %param.3), kind=kLoop, calls=%fused_computation.71 | loop fusion | flops 18874368 | bytes 40894464 | tf_op jit(solution)/shard_map/sub | solution.py:67
  491.9 56.7 %all-to-all-done.1 = f32[2,5,4,192,512]{4,3,2,1,0:T(8,128)} async-done(((f32[2,5,4,192,512]{4,3,2,1,0:T(8,128)}), f32[2,5,4,192,512]{4,3,2,1,0:T(8,128)}, u32[]{:S(2)}, u32[]{:S(2)}) %all-to-all-start.1) | async-done | bytes 15728672 | tf_op jit(solution)/shard_map/all_to_all | solution.py:107
  548.6 11.9 %slice_bitcast_fusion.6 = (f32[2,1,4,24,8,512]{5,4,3,2,1,0:T(8,128)}, f32[2,1,4,24,8,512]{5,4,3,2,1,0:T(8,128)}, f32[2,1,4,24,8,512]{5,4,3,2,1,0:T(8,128)}, f32[...) fusion(f32[5,4,192,2,512]{4,2,1,0,3:T(8,128)} %bitcast.8), kind=kLoop, calls=%fused_computation.56 | loop fusion | bytes 31457280
  560.5 2.4 copy.18
  562.9 2.4 copy.19
  565.4 0.4 copy.20
  565.7 0.4 copy.21
  566.1 2.0 copy.22
  568.1 1.4 slice-done.1
  569.8 8.3 %multiply_add_fusion.2 = (f32[1,4,192,1024]{3,2,1,0:T(8,128)}, f32[1,4,192,1024]{3,2,1,0:T(8,128)}, f32[1,4,192,1024]{3,2,1,0:T(8,128)}) fusion(f32[1,4,192,1024]{3,2,1,0:T(8,128)S(1)} %bitcast.36, f32[1,4,192,1024]{3,2,1,0:T(8,128)S(1)} %bitcast.35, f32[3,4,192,1024]{3,2,1,0:T(8,128)S(1)} %bitcast.33, f32[3,4,192,1024]{3,2,1,0:T(8,128)} %param.3, ...), kind=kLoop, calls=%fused_computation.75 | loop fusion | flops 11010048 | bytes 34603008 | tf_op jit(solution)/shard_map/add | solution.py:56
  578.1 11.9 %fusion.26 = f32[3,4,192,1024]{3,2,1,0:T(8,128)} fusion(f32[3,4,192,1024]{3,2,1,0:T(8,128)S(1)} %bitcast.33, f32[1,4,192,1024]{3,2,1,0:T(8,128)} %get-tuple-element.6, f32[1,4,192,1024]{3,2,1,0:T(8,128)} %fusion.33, f32[1,4,192,1024]{3,2,1,0:T(8,128)} %get-tuple-element.5, f32[1,4,192,1024]{3,2,1,0:T(8,128)} %get-tuple-element.9, ...), kind=kLoop, calls=%fused_computation.48 | loop fusion | flops 16515072 | bytes 37749504 | tf_op jit(solution)/shard_map/add | solution.py:118
  (20 shorter events, 0.3 us)
Async XLA Ops:
  0.0 5.5 copy-start
  5.5 7.4 %copy-start.2 = (f32[2,4,192,1024]{3,2,1,0:T(8,128)}, f32[2,4,192,1024]{3,2,1,0:T(8,128)S(1)}, u32[]{:S(2)}) copy-start(f32[2,4,192,1024]{3,2,1,0:T(8,128)S(1)} %slice.149) | copy-start | bytes 18874372
  12.9 364.4 %collective-permute-start = (f32[5,4,192,1024]{3,2,1,0:T(8,128)}, f32[5,4,192,1024]{3,2,1,0:T(8,128)}, u32[]{:S(2)}, u32[]{:S(2)}) collective-permute-start(f32[5,4,192,1024]{3,2,1,0:T(8,128)} %pad_maximum_fusion.1), channel_id=1, source_target_pairs={{2,0},{4,2},{6,4},{8,6},{10,8},{12,10},{14,12},{16,14},{18,16},{20... | collective-permute-start | bytes 47185928 | tf_op jit(solution)/shard_map/ppermute | solution.py:21
  13.7 363.6 %collective-permute-start.1 = (f32[5,4,192,1024]{3,2,1,0:T(8,128)}, f32[5,4,192,1024]{3,2,1,0:T(8,128)}, u32[]{:S(2)}, u32[]{:S(2)}) collective-permute-start(f32[5,4,192,1024]{3,2,1,0:T(8,128)} %pad_maximum_fusion.1), channel_id=1, source_target_pairs={{0,2},{2,4},{4,6},{6,8},{8,10},{10,12},{12,14},{14,16},{16,18},{18... | collective-permute-start | bytes 47185928 | tf_op jit(solution)/shard_map/ppermute | solution.py:20
  35.5 239.6 %all-to-all-start = ((f32[5,4,192,1024]{2,1,0,3:T(4,128)}), f32[5,4,192,1024]{2,1,0,3:T(4,128)}, u32[]{:S(2)}, u32[]{:S(2)}) async-start(f32[5,4,192,1024]{2,1,0,3:T(4,128)} %copy.10), calls=%async_computation | async-start | bytes 41943040 | tf_op jit(solution)/shard_map/all_to_all | solution.py:103
  367.8 180.8 %all-to-all-start.1 = ((f32[2,5,4,192,512]{4,3,2,1,0:T(8,128)}), f32[2,5,4,192,512]{4,3,2,1,0:T(8,128)}, u32[]{:S(2)}, u32[]{:S(2)}) async-start(f32[2,5,4,192,512]{4,3,2,1,0:T(8,128)} %pad_maximum_fusion.2), calls=%async_computation.1 | async-start | bytes 31457280 | tf_op jit(solution)/shard_map/all_to_all | solution.py:107
  465.8 14.7 %copy-start.1 = (f32[5,4,192,1024]{3,2,1,0:T(8,128)S(1)}, f32[5,4,192,1024]{3,2,1,0:T(8,128)}, u32[]{:S(2)}) copy-start(f32[5,4,192,1024]{3,2,1,0:T(8,128)} %fusion.3) | copy-start | bytes 47185924
  560.5 5.2 copy-start.4
  562.9 3.2 copy-start.3
  562.9 5.2 slice-start
  565.3 4.2 slice-start.1
  565.7 4.0 slice-start.2
  569.8 8.3 %copy-start.5 = (f32[192]{0:T(256)S(1)}, f32[192]{0:T(256)}, u32[]{:S(2)}) copy-start(f32[192]{0:T(256)} %add_multiply_fusion) | copy-start | bytes 2308
